TPU v7x, 32 devices: a whole 2x2x4 slice. The times are simulated.
32 devices in a mesh: rep: 8 (over y, x, core), shard: 4 (over z).
Axes of the slice: x: 2, y: 2, z: 4, core: 2. Of those that a mesh axis runs over, the one named last changes fastest.
Arguments:
- gradients: bfloat16 [8, 96, 2560], P(None, 'shard')
- momentum: float32 [8, 96, 2560], P(None, 'shard'), may hold values from -60 to 60
Outputs:
- updates: bfloat16 [8, 96, 2560], P(None, 'shard', 'rep')
- new_momentum: float32 [8, 96, 2560], P(None, 'shard')
All inputs are finite; a program needn't handle non-finite values.
Results may differ from a plain program's by a relative error of at most 0.0014.
Values may be sent and summed in bfloat16 or wider, within the bound.
A program may use at most 64 MiB of HBM per device.

v0:
```python
import math
import jax
import jax.numpy as jnp
from jax import lax
from jax.sharding import PartitionSpec as P

ITERS = 5
momentum_decay = 0.95
norm_floor = 1e-07
quintic_terms = (3.4445, -4.775, 2.0315)


def mm(a, b):
    return jnp.einsum("kij,kjl->kil", a, b, precision=lax.Precision.HIGHEST)


def schulz_factor(gram, scale):
    total = jnp.trace(gram, axis1=1, axis2=2)[:, None, None]
    inverse = 1.0 / (jnp.sqrt(total) + norm_floor)
    g = jnp.where(inverse > 0, gram * inverse * inverse, 0.0)
    eye = jnp.eye(gram.shape[-1], dtype=jnp.float32)
    a, b, c = quintic_terms
    q = None
    for turn in range(ITERS):
        poly = a * eye + b * g + c * mm(g, g)
        q = poly if q is None else mm(poly, q)
        if turn < ITERS - 1:
            g = mm(poly, mm(poly, g))
    return q * (scale * inverse)


def per_device_plain(gradients, momentum):
    rows, width = gradients.shape[1:]
    scale = 0.2 * math.sqrt(max(rows * lax.axis_size("shard"), width))
    replicas = lax.axis_size("rep")
    grads = gradients.astype(jnp.float32)
    new_momentum = momentum_decay * momentum + grads
    effective = grads + momentum_decay * new_momentum
    cols = width // replicas
    mine = lax.dynamic_slice_in_dim(effective, lax.axis_index("rep") * cols, cols, 2)
    whole = lax.all_to_all(mine, "shard", split_axis=0, concat_axis=1, tiled=True)
    gram = jnp.einsum("kij,klj->kil", whole, whole, precision=lax.Precision.HIGHEST)
    factor = schulz_factor(lax.psum(gram, "rep"), scale)
    out = mm(factor, whole).astype(jnp.bfloat16)
    return (lax.all_to_all(out, "shard", split_axis=1, concat_axis=0, tiled=True), new_momentum)


def solution(mesh):
    in_specs = (P(None, "shard", None), P(None, "shard", None))
    out_specs = (P(None, "shard", "rep"), P(None, "shard", None))
    return jax.shard_map(
        per_device_plain, mesh=mesh, in_specs=in_specs, out_specs=out_specs, check_vma=False
    )
```

profile of v0, /device:TPU:0, one launch (start us, length us, event | category | flops | bytes accessed | tf_op | source)
XLA Modules:
  0.0 107.0 jit_solution(3335476174348482193)
XLA Ops:
  7.2 2.9 %convert_element_type.7 = f32[8,24,2560]{2,1,0:T(8,128)} convert(bf16[8,24,2560]{2,1,0:T(8,128)(2,1)} %param.2) | non-fusion elementwise | flops 491520 | bytes 2949120 | tf_op jit(solution)/shard_map/convert_element_type | solution.py:36
  10.1 0.3 multiply_add_fusion
  10.3 2.2 %dynamic-slice_add_fusion = f32[8,24,320]{2,1,0:T(8,128)} fusion(f32[8,24,2560]{2,1,0:T(8,128)} %convert_element_type.7, s32[]{:T(128)S(6)} %select_n.12, f32[8,24,2560]{2,1,0:T(8,128)S(1)} %multiply_add_fusion), kind=kLoop, calls=%fused_computation.13 | loop fusion | flops 122880 | bytes 737284 | tf_op jit(solution)/shard_map/add | solution.py:38
  12.6 6.3 %all-to-all-start = ((f32[8,24,320]{2,1,0:T(8,128)}), f32[8,24,320]{2,1,0:T(8,128)S(1)}, u32[]{:S(2)}, u32[]{:S(2)}) async-start(f32[8,24,320]{2,1,0:T(8,128)} %dynamic-slice_add_fusion), calls=%async_computation | async-start | bytes 589824 | tf_op jit(solution)/shard_map/all_to_all | solution.py:41
  18.9 9.6 %all-to-all-done = f32[8,24,320]{2,1,0:T(8,128)S(1)} async-done(((f32[8,24,320]{2,1,0:T(8,128)}), f32[8,24,320]{2,1,0:T(8,128)S(1)}, u32[]{:S(2)}, u32[]{:S(2)}) %all-to-all-start) | async-done | bytes 245792 | tf_op jit(solution)/shard_map/all_to_all | solution.py:41
  28.5 1.1 %fusion.14 = f32[2,96,96]{2,1,0:T(8,128)} fusion(f32[2,96,320]{2,1,0:T(8,128)S(1)} %bitcast.43), kind=kOutput, calls=%fused_computation.31 | convolution fusion | flops 70778880 | bytes 319488 | tf_op jit(solution)/shard_map/kij,klj->kil/dot_general | solution.py:42
  29.7 50.6 %all-reduce.2.cloned.1.call-done = f32[2,96,96]{2,1,0:T(8,128)} async-done(((f32[2,96,96]{2,1,0:T(8,128)}), f32[2,96,96]{2,1,0:T(8,128)}) %all-reduce.2.cloned.1.call-update) | async-done | bytes 73744 | tf_op jit(solution)/shard_map/psum | solution.py:43
  80.3 1.0 select_reduce_fusion
  81.3 1.4 %fusion = f32[2,96,96]{2,1,0:T(8,128)S(1)} fusion(f32[2,96,96]{2,1,0:T(8,128)} %all-reduce.2.cloned.1.call-done, f32[2]{0:T(128)S(1)} %get-tuple-element.3, f32[96,96]{1,0:T(8,128)S(1)} %broadcast_select_fusion, pred[2]{0:T(512)(128)(4,1)S(1)} %broadcast_compare_fusion), kind=kOutput, calls=%fused_computation.8 | convolution fusion | flops 21417984 | bytes 184330 | tf_op jit(solution)/shard_map/kij,kjl->kil/dot_general | solution.py:14
  82.7 1.2 %fusion.5 = f32[2,96,96]{2,1,0:T(8,128)S(1)} fusion(f32[2,96,96]{2,1,0:T(8,128)S(1)} %fusion, f32[2,96,96]{2,1,0:T(8,128)} %all-reduce.2.cloned.1.call-done, f32[2]{0:T(128)S(1)} %get-tuple-element.3, pred[2]{0:T(512)(128)(4,1)S(1)} %broadcast_compare_fusion), kind=kOutput, calls=%fused_computation.17 | convolution fusion | flops 21288960 | bytes 221194 | tf_op jit(solution)/shard_map/kij,kjl->kil/dot_general | solution.py:14
  83.9 0.2 fusion.15
  84.1 0.2 fusion.1
  84.6 0.2 fusion.16
  85.1 0.2 fusion.2
  85.4 0.2 fusion.18
  85.6 0.2 fusion.23
  85.8 0.2 fusion.19
  86.1 0.2 fusion.3
  86.5 0.2 fusion.24
  87.0 0.2 fusion.4
  87.3 0.2 convolution_multiply_fusion
  87.5 0.4 convolution_convert_fusion
  88.0 11.5 %all_to_all.36 = bf16[2,96,320]{2,0,1:T(2,128)(2,1)S(1)} all-to-all(bf16[2,96,320]{2,0,1:T(2,128)(2,1)S(1)} %copy.7), channel_id=1, replica_groups=mesh['rep'=8,'shard'=4] {'shard'}, dimensions={1} | all-to-all | bytes 245760 | tf_op jit(solution)/shard_map/all_to_all | solution.py:45
  99.5 0.7 copy.8
  (18 shorter events, 1.1 us)
Async XLA Ops:
  7.2 2.9 %copy-start = (bf16[8,24,2560]{2,1,0:T(8,128)(2,1)S(1)}, bf16[8,24,2560]{2,1,0:T(8,128)(2,1)}, u32[]{:S(2)}) copy-start(bf16[8,24,2560]{2,1,0:T(8,128)(2,1)} %param.2) | copy-start | bytes 2949124
  7.2 2.9 %copy-start.2 = (f32[8,24,2560]{2,1,0:T(8,128)S(1)}, f32[8,24,2560]{2,1,0:T(8,128)}, u32[]{:S(2)}) copy-start(f32[8,24,2560]{2,1,0:T(8,128)} %param.3) | copy-start | bytes 5898244
  10.3 74.1 %copy-start.1 = (f32[8,24,2560]{2,1,0:T(8,128)}, f32[8,24,2560]{2,1,0:T(8,128)S(1)}, u32[]{:S(2)}) copy-start(f32[8,24,2560]{2,1,0:T(8,128)S(1)} %multiply_add_fusion) | copy-start | bytes 5898244
  12.6 15.9 %all-to-all-start = ((f32[8,24,320]{2,1,0:T(8,128)}), f32[8,24,320]{2,1,0:T(8,128)S(1)}, u32[]{:S(2)}, u32[]{:S(2)}) async-start(f32[8,24,320]{2,1,0:T(8,128)} %dynamic-slice_add_fusion), calls=%async_computation | async-start | bytes 589824 | tf_op jit(solution)/shard_map/all_to_all | solution.py:41
  18.9 61.4 %all-reduce.2.cloned.1.call-start = ((), (), s32[]{:S(2)}) async-start(), calls=%async_computation.2 | async-start | bytes 196608 | tf_op jit(solution)/shard_map/psum | solution.py:43
Sparse Core Ops, SparseCore 0:
  29.8 50.4 all-reduce.1
where the time goes:
time: 107 us
  waiting for transfers between devices  60.2 us (56%)
  between operations  14.2 us (13%)
  blocking collectives  11.5 us (11%)
  matrix products  7.54 us (7%)
  other arithmetic  6.41 us (6%)
  starting transfers between devices  6.32 us (6%)
    psum x1, waiting for transfers between devices, per_device_plain(): factor = schulz_factor(lax.psum(gram, 'rep'), scale)  50.6 us
    all_to_all x1, blocking collectives, per_device_plain(): lax.all_to_all(out, 'shard', split_axis=1, concat_axis=0, tiled=True)  11.5 us
    all_to_all x1, waiting for transfers between devices, per_device_plain(): lax.all_to_all(mine, 'shard', split_axis=0, concat_axis=1, tiled=True)  9.6 us
    dot_general x18, matrix products, mm(): return jnp.einsum('kij,kjl->kil', a, b, precision=lax.Precision.HIGHEST)  6.43 us
    all_to_all x1, starting transfers between devices, per_device_plain(): lax.all_to_all(mine, 'shard', split_axis=0, concat_axis=1, tiled=True)  6.32 us
    convert_element_type x1, other arithmetic, per_device_plain(): grads = gradients.astype(jnp.float32)  2.87 us
    add x1, other arithmetic, per_device_plain(): effective = grads + momentum_decay * new_momentum  2.25 us
  transfers between devices with their start and end apart: 2, of which 2 were waited for; matrix products, arithmetic and copies ran while one was open for 0% of the time, Pallas kernels for 0%

commit v1 on v0

--- a/solution.py
+++ b/solution.py
@@ -8,6 +8,12 @@
 momentum_decay = 0.95
 norm_floor = 1e-07
 quintic_terms = (3.4445, -4.775, 2.0315)
+
+
+def add_all(block, mesh_axis):
+    blocks = lax.all_gather(block, mesh_axis, axis=0, tiled=False)
+    result = blocks.sum(axis=0)
+    return result
 
 
 def mm(a, b):
@@ -40,7 +46,7 @@
     mine = lax.dynamic_slice_in_dim(effective, lax.axis_index("rep") * cols, cols, 2)
     whole = lax.all_to_all(mine, "shard", split_axis=0, concat_axis=1, tiled=True)
     gram = jnp.einsum("kij,klj->kil", whole, whole, precision=lax.Precision.HIGHEST)
-    factor = schulz_factor(lax.psum(gram, "rep"), scale)
+    factor = schulz_factor(add_all(gram, "rep"), scale)
     out = mm(factor, whole).astype(jnp.bfloat16)
     return (lax.all_to_all(out, "shard", split_axis=1, concat_axis=0, tiled=True), new_momentum)
 

time: 107 us -> 48.4 us (0.45)
  waiting for transfers between devices: 60.2 us -> 9.59 us
  between operations: 14.2 us -> 0.85 us
  blocking collectives: 11.5 us -> 20 us
  matrix products: 7.54 us -> 4.94 us
    psum x1 -> x0, waiting for transfers between devices: 50.6 us -> none  [per_device_plain(): factor = schulz_factor(lax.psum(gram, 'rep'), scale)]
    all_gather x0 -> x1, blocking collectives: none -> 10.4 us  [add_all(): blocks = lax.all_gather(block, mesh_axis, axis=0, tiled=False)]
    dot_general x18, matrix products: 6.43 us -> 4.48 us  [mm(): return jnp.einsum('kij,kjl->kil', a, b, precision=lax.Precision.HIGHEST)]
    all_to_all x1, blocking collectives: 11.5 us -> 9.6 us  [per_device_plain(): lax.all_to_all(out, 'shard', split_axis=1, concat_axis=0, tiled=True)]
  transfers between devices with their start and end apart: 2 -> 1, of which waited for: 2 -> 1; matrix products, arithmetic and copies ran while one was open for 0% -> 0% of each run, Pallas kernels for 0% -> 0%
where the time goes in v1:
time: 48.4 us; the launch traced here: 48.1 us
  blocking collectives  20 us (41%)
  waiting for transfers between devices  9.59 us (20%)
  starting transfers between devices  6.32 us (13%)
  other arithmetic  5.56 us (11%)
  matrix products  4.94 us (10%)
  between operations  0.85 us (2%)
  local copies, waits for them, and re-layouts  0.83 us (2%)
    all_gather x1, blocking collectives, add_all(): blocks = lax.all_gather(block, mesh_axis, axis=0, tiled=False)  10.4 us
    all_to_all x1, blocking collectives, per_device_plain(): lax.all_to_all(out, 'shard', split_axis=1, concat_axis=0, tiled=True)  9.6 us
    all_to_all x1, waiting for transfers between devices, per_device_plain(): lax.all_to_all(mine, 'shard', split_axis=0, concat_axis=1, tiled=True)  9.59 us
    all_to_all x1, starting transfers between devices, per_device_plain(): lax.all_to_all(mine, 'shard', split_axis=0, concat_axis=1, tiled=True)  6.32 us
    dot_general x18, matrix products, mm(): return jnp.einsum('kij,kjl->kil', a, b, precision=lax.Precision.HIGHEST)  4.48 us
    convert_element_type x1, other arithmetic, per_device_plain(): grads = gradients.astype(jnp.float32)  2.85 us
    add x1, other arithmetic, per_device_plain(): effective = grads + momentum_decay * new_momentum  2.24 us
  transfers between devices with their start and end apart: 1, of which 1 were waited for; matrix products, arithmetic and copies ran while one was open for 0% of the time, Pallas kernels for 0%

profile of v1, /device:TPU:0, one launch (start us, length us, event | category | flops | bytes accessed | tf_op | source)
XLA Modules:
  0.0 48.1 jit_solution(4712804642404557580)
XLA Ops:
  0.7 2.9 %convert_element_type.7 = f32[8,24,2560]{2,1,0:T(8,128)} convert(bf16[8,24,2560]{2,1,0:T(8,128)(2,1)} %param.2) | non-fusion elementwise | flops 491520 | bytes 2949120 | tf_op jit(solution)/shard_map/convert_element_type | solution.py:42
  3.5 0.3 multiply_add_fusion
  3.8 2.2 %dynamic-slice_add_fusion = f32[8,24,320]{2,1,0:T(8,128)} fusion(f32[8,24,2560]{2,1,0:T(8,128)} %convert_element_type.7, s32[]{:T(128)S(6)} %select_n.12, f32[8,24,2560]{2,1,0:T(8,128)S(1)} %multiply_add_fusion), kind=kLoop, calls=%fused_computation.13 | loop fusion | flops 122880 | bytes 737284 | tf_op jit(solution)/shard_map/add | solution.py:44
  6.0 6.3 %all-to-all-start = ((f32[8,24,320]{2,1,0:T(8,128)}), f32[8,24,320]{2,1,0:T(8,128)S(1)}, u32[]{:S(2)}, u32[]{:S(2)}) async-start(f32[8,24,320]{2,1,0:T(8,128)} %dynamic-slice_add_fusion), calls=%async_computation | async-start | bytes 589824 | tf_op jit(solution)/shard_map/all_to_all | solution.py:47
  12.4 9.6 %all-to-all-done = f32[8,24,320]{2,1,0:T(8,128)S(1)} async-done(((f32[8,24,320]{2,1,0:T(8,128)}), f32[8,24,320]{2,1,0:T(8,128)S(1)}, u32[]{:S(2)}, u32[]{:S(2)}) %all-to-all-start) | async-done | bytes 245792 | tf_op jit(solution)/shard_map/all_to_all | solution.py:47
  22.0 0.5 fusion.14
  22.5 10.4 %all-gather = f32[16,96,96]{2,1,0:T(8,128)S(1)} all-gather(f32[2,96,96]{2,1,0:T(8,128)S(1)} %fusion.14), channel_id=2, replica_groups=mesh['rep'=8,'shard'=4] {'rep'}, dimensions={0}, use_global_device_ids=true | all-gather | bytes 663552 | tf_op jit(solution)/shard_map/all_gather | solution.py:14
  33.1 0.3 fusion
  33.4 0.3 fusion.5
  33.7 0.2 fusion.15
  34.0 0.2 fusion.1
  34.2 0.2 fusion.22
  34.4 0.2 fusion.16
  34.7 0.2 fusion.17
  34.9 0.2 fusion.2
  35.2 0.2 fusion.18
  35.4 0.2 fusion.23
  35.9 0.2 fusion.3
  36.6 0.2 fusion.21
  36.8 0.2 fusion.4
  37.1 0.2 convolution_multiply_fusion
  37.3 0.4 convolution_convert_fusion
  37.8 9.6 %all_to_all.36 = bf16[2,96,320]{2,0,1:T(2,128)(2,1)S(1)} all-to-all(bf16[2,96,320]{2,0,1:T(2,128)(2,1)S(1)} %copy.7), channel_id=1, replica_groups=mesh['rep'=8,'shard'=4] {'shard'}, dimensions={1} | all-to-all | bytes 245760 | tf_op jit(solution)/shard_map/all_to_all | solution.py:51
  47.4 0.7 %copy.8 = bf16[4,2,24,320]{3,2,1,0:T(8,128)(2,1)} copy(bf16[4,2,24,320]{3,1,2,0:T(2,128)(2,1)S(1)} %bitcast.48) | data formatting | bytes 245760 | tf_op jit(solution)/shard_map/all_to_all | solution.py:51
  (17 shorter events, 1.0 us)
Async XLA Ops:
  0.6 2.9 %copy-start = (bf16[8,24,2560]{2,1,0:T(8,128)(2,1)S(1)}, bf16[8,24,2560]{2,1,0:T(8,128)(2,1)}, u32[]{:S(2)}) copy-start(bf16[8,24,2560]{2,1,0:T(8,128)(2,1)} %param.2) | copy-start | bytes 2949124
  0.6 2.9 %copy-start.2 = (f32[8,24,2560]{2,1,0:T(8,128)S(1)}, f32[8,24,2560]{2,1,0:T(8,128)}, u32[]{:S(2)}) copy-start(f32[8,24,2560]{2,1,0:T(8,128)} %param.3) | copy-start | bytes 5898244
  3.8 29.2 %copy-start.1 = (f32[8,24,2560]{2,1,0:T(8,128)}, f32[8,24,2560]{2,1,0:T(8,128)S(1)}, u32[]{:S(2)}) copy-start(f32[8,24,2560]{2,1,0:T(8,128)S(1)} %multiply_add_fusion) | copy-start | bytes 5898244
  6.0 15.9 %all-to-all-start = ((f32[8,24,320]{2,1,0:T(8,128)}), f32[8,24,320]{2,1,0:T(8,128)S(1)}, u32[]{:S(2)}, u32[]{:S(2)}) async-start(f32[8,24,320]{2,1,0:T(8,128)} %dynamic-slice_add_fusion), calls=%async_computation | async-start | bytes 589824 | tf_op jit(solution)/shard_map/all_to_all | solution.py:47

commit v2 on v0

--- a/solution.py
+++ b/solution.py
@@ -38,7 +38,15 @@
     effective = grads + momentum_decay * new_momentum
     cols = width // replicas
     mine = lax.dynamic_slice_in_dim(effective, lax.axis_index("rep") * cols, cols, 2)
-    whole = lax.all_to_all(mine, "shard", split_axis=0, concat_axis=1, tiled=True)
+    whole = jnp.concatenate(
+        jax.lax.all_to_all(
+            jnp.stack(jnp.split(mine, jax.lax.axis_size("shard"), axis=0)),
+            axis_name="shard",
+            split_axis=0,
+            concat_axis=0,
+        ),
+        axis=1,
+    )
     gram = jnp.einsum("kij,klj->kil", whole, whole, precision=lax.Precision.HIGHEST)
     factor = schulz_factor(lax.psum(gram, "rep"), scale)
     out = mm(factor, whole).astype(jnp.bfloat16)

time: 107 us -> 107 us (level)
  no operation moved by 1% of the time
where the time goes in v2:
time: 107 us
  waiting for transfers between devices  60.2 us (56%)
  between operations  14.2 us (13%)
  blocking collectives  11.5 us (11%)
  matrix products  7.54 us (7%)
  other arithmetic  6.43 us (6%)
  starting transfers between devices  6.32 us (6%)
    psum x1, waiting for transfers between devices, per_device_plain(): factor = schulz_factor(lax.psum(gram, 'rep'), scale)  50.6 us
    all_to_all x1, blocking collectives, per_device_plain(): lax.all_to_all(out, 'shard', split_axis=1, concat_axis=0, tiled=True)  11.5 us
    all_to_all x1, waiting for transfers between devices, per_device_plain(): jax.lax.all_to_all(jnp.stack(jnp.split(mine, jax.lax.axis_size('shard'),...  9.6 us
    dot_general x18, matrix products, mm(): return jnp.einsum('kij,kjl->kil', a, b, precision=lax.Precision.HIGHEST)  6.43 us
    all_to_all x1, starting transfers between devices, per_device_plain(): jax.lax.all_to_all(jnp.stack(jnp.split(mine, jax.lax.axis_size('shard'),...  6.32 us
    convert_element_type x1, other arithmetic, per_device_plain(): grads = gradients.astype(jnp.float32)  2.86 us
  transfers between devices with their start and end apart: 2, of which 2 were waited for; matrix products, arithmetic and copies ran while one was open for 0% of the time, Pallas kernels for 0%

profile of v2, /device:TPU:0, one launch (start us, length us, event | category | flops | bytes accessed | tf_op | source)
XLA Modules:
  0.0 107.0 jit_solution(12393420851496176867)
XLA Ops:
  7.2 2.9 %convert_element_type.7 = f32[8,24,2560]{2,1,0:T(8,128)} convert(bf16[8,24,2560]{2,1,0:T(8,128)(2,1)} %param.2) | non-fusion elementwise | flops 491520 | bytes 2949120 | tf_op jit(solution)/shard_map/convert_element_type | solution.py:36
  10.1 0.3 multiply_add_fusion
  10.3 1.5 %dynamic-slice_add_fusion = f32[8,24,320]{2,1,0:T(8,128)S(1)} fusion(f32[8,24,2560]{2,1,0:T(8,128)} %convert_element_type.7, s32[]{:T(128)S(6)} %select_n.12, f32[8,24,2560]{2,1,0:T(8,128)S(1)} %multiply_add_fusion), kind=kLoop, calls=%fused_computation.13 | loop fusion | flops 122880 | bytes 737284 | tf_op jit(solution)/shard_map/add | solution.py:38
  11.9 0.7 pad_maximum_fusion
  12.6 6.3 %all-to-all-start = ((f32[4,2,24,320]{3,2,1,0:T(8,128)}), f32[4,2,24,320]{3,2,1,0:T(8,128)S(1)}, u32[]{:S(2)}, u32[]{:S(2)}) async-start(f32[4,2,24,320]{3,2,1,0:T(8,128)} %pad_maximum_fusion), calls=%async_computation | async-start | bytes 589824 | tf_op jit(solution)/shard_map/all_to_all | solution.py:42
  19.0 9.6 %all-to-all-done = f32[4,2,24,320]{3,2,1,0:T(8,128)S(1)} async-done(((f32[4,2,24,320]{3,2,1,0:T(8,128)}), f32[4,2,24,320]{3,2,1,0:T(8,128)S(1)}, u32[]{:S(2)}, u32[]{:S(2)}) %all-to-all-start) | async-done | bytes 245792 | tf_op jit(solution)/shard_map/all_to_all | solution.py:42
  28.6 1.1 %fusion.14 = f32[2,96,96]{2,1,0:T(8,128)} fusion(f32[2,96,320]{2,1,0:T(8,128)S(1)} %bitcast.49), kind=kOutput, calls=%fused_computation.36 | convolution fusion | flops 70778880 | bytes 319488 | tf_op jit(solution)/shard_map/kij,klj->kil/dot_general | solution.py:50
  29.8 50.6 %all-reduce.2.cloned.1.call-done = f32[2,96,96]{2,1,0:T(8,128)} async-done(((f32[2,96,96]{2,1,0:T(8,128)}), f32[2,96,96]{2,1,0:T(8,128)}) %all-reduce.2.cloned.1.call-update) | async-done | bytes 73744 | tf_op jit(solution)/shard_map/psum | solution.py:51
  80.3 1.0 select_reduce_fusion
  81.4 1.4 %fusion = f32[2,96,96]{2,1,0:T(8,128)S(1)} fusion(f32[2,96,96]{2,1,0:T(8,128)} %all-reduce.2.cloned.1.call-done, f32[2]{0:T(128)S(1)} %get-tuple-element.3, f32[96,96]{1,0:T(8,128)S(1)} %broadcast_select_fusion, pred[2]{0:T(512)(128)(4,1)S(1)} %broadcast_compare_fusion), kind=kOutput, calls=%fused_computation.8 | convolution fusion | flops 21417984 | bytes 184330 | tf_op jit(solution)/shard_map/kij,kjl->kil/dot_general | solution.py:14
  82.8 1.2 %fusion.5 = f32[2,96,96]{2,1,0:T(8,128)S(1)} fusion(f32[2,96,96]{2,1,0:T(8,128)S(1)} %fusion, f32[2,96,96]{2,1,0:T(8,128)} %all-reduce.2.cloned.1.call-done, f32[2]{0:T(128)S(1)} %get-tuple-element.3, pred[2]{0:T(512)(128)(4,1)S(1)} %broadcast_compare_fusion), kind=kOutput, calls=%fused_computation.18 | convolution fusion | flops 21288960 | bytes 221194 | tf_op jit(solution)/shard_map/kij,kjl->kil/dot_general | solution.py:14
  84.0 0.2 fusion.15
  84.2 0.2 fusion.1
  84.4 0.2 fusion.22
  84.7 0.2 fusion.16
  84.9 0.2 fusion.17
  85.2 0.2 fusion.2
  85.4 0.2 fusion.18
  86.1 0.2 fusion.3
  87.1 0.2 fusion.4
  87.3 0.2 convolution_multiply_fusion
  87.5 0.4 convolution_convert_fusion
  88.1 11.5 %all_to_all.23 = bf16[2,96,320]{2,0,1:T(2,128)(2,1)S(1)} all-to-all(bf16[2,96,320]{2,0,1:T(2,128)(2,1)S(1)} %copy.7), channel_id=1, replica_groups=mesh['rep'=8,'shard'=4] {'shard'}, dimensions={1} | all-to-all | bytes 245760 | tf_op jit(solution)/shard_map/all_to_all | solution.py:53
  99.5 0.7 copy.8
  (20 shorter events, 1.4 us)
Async XLA Ops:
  7.2 2.9 %copy-start = (bf16[8,24,2560]{2,1,0:T(8,128)(2,1)S(1)}, bf16[8,24,2560]{2,1,0:T(8,128)(2,1)}, u32[]{:S(2)}) copy-start(bf16[8,24,2560]{2,1,0:T(8,128)(2,1)} %param.2) | copy-start | bytes 2949124
  7.2 2.9 %copy-start.2 = (f32[8,24,2560]{2,1,0:T(8,128)S(1)}, f32[8,24,2560]{2,1,0:T(8,128)}, u32[]{:S(2)}) copy-start(f32[8,24,2560]{2,1,0:T(8,128)} %param.3) | copy-start | bytes 5898244
  10.3 19.4 %copy-start.1 = (f32[8,24,2560]{2,1,0:T(8,128)}, f32[8,24,2560]{2,1,0:T(8,128)S(1)}, u32[]{:S(2)}) copy-start(f32[8,24,2560]{2,1,0:T(8,128)S(1)} %multiply_add_fusion) | copy-start | bytes 5898244
  12.6 15.9 %all-to-all-start = ((f32[4,2,24,320]{3,2,1,0:T(8,128)}), f32[4,2,24,320]{3,2,1,0:T(8,128)S(1)}, u32[]{:S(2)}, u32[]{:S(2)}) async-start(f32[4,2,24,320]{3,2,1,0:T(8,128)} %pad_maximum_fusion), calls=%async_computation | async-start | bytes 589824 | tf_op jit(solution)/shard_map/all_to_all | solution.py:42
  19.0 61.4 %all-reduce.2.cloned.1.call-start = ((), (), s32[]{:S(2)}) async-start(), calls=%async_computation.2 | async-start | bytes 196608 | tf_op jit(solution)/shard_map/psum | solution.py:51
Sparse Core Ops, SparseCore 0:
  29.9 50.4 all-reduce.1
